TPU v7x, 32 devices: a whole 2x2x4 slice. The times are simulated.
32 devices in a mesh: dp: 8 (over y, x, core), seq: 4 (over z).
Axes of the slice: x: 2, y: 2, z: 4, core: 2. Of those that a mesh axis runs over, the one named last changes fastest.
Arguments:
- tokens: bfloat16 [16, 1024, 1024], P('dp', 'seq'), may hold values from -17 to 17
- positions: int32 [16, 1024], P('dp', 'seq'), may hold values from 0 to 4092, as said below
- cotangent: bfloat16 [16, 1024, 1024], P('dp', 'seq'), may hold values from -6 to 6
- q_weight: bfloat16 [1024, 1024], P('dp'), may hold values from -0.1875 to 0.1875
- key_matrix: bfloat16 [1024, 512], P('dp'), may hold values from -0.1875 to 0.1875
- value_matrix: bfloat16 [1024, 512], P('dp'), may hold values from -0.1875 to 0.1875
- out_weight: bfloat16 [1024, 1024], P('dp'), may hold values from -2 to 2
- gate_weight: bfloat16 [1024, 4608], P('dp'), may hold values from -0.1875 to 0.1875
- up_weight: bfloat16 [1024, 4608], P('dp'), may hold values from -0.1875 to 0.1875
- down_weight: bfloat16 [1024, 4608], P('dp'), may hold values from -0.375 to 0.375
- attn_gain: float32 [1024], replicated, may hold values from 0.1 to 1.9
- ffn_gain: float32 [1024], replicated, may hold values from 0.1 to 1.9
- q_gain: float32 [64], replicated, may hold values from 0.1 to 1.9
- k_gain: float32 [64], replicated, may hold values from 0.1 to 1.9
Outputs:
- output: bfloat16 [16, 1024, 1024], P('dp', 'seq')
- input_grad: bfloat16 [16, 1024, 1024], P('dp', 'seq')
- q_weight_grad: float32 [1024, 1024], P('dp')
- k_weight_grad: float32 [1024, 512], P('dp')
- v_weight_grad: float32 [1024, 512], P('dp')
- out_weight_grad: float32 [1024, 1024], P('dp')
- gate_weight_grad: float32 [1024, 4608], P('dp')
- up_weight_grad: float32 [1024, 4608], P('dp')
- down_weight_grad: float32 [1024, 4608], P('dp')
- attn_gain_grad: float32 [1024], replicated
- ffn_gain_grad: float32 [1024], replicated
- q_gain_grad: float32 [64], replicated
- k_gain_grad: float32 [64], replicated
Inputs may be any that keep to these rules, and one draw needn't show every extreme that they name: Along each sequence the positions rise by 1 to 4 from one token to the next, the first being 0; in one sequence every step is 4.
All inputs are finite; a program needn't handle non-finite values.
Results may differ from a plain program's by a relative error of at most 0.02.
Values may be sent and summed in bfloat16 or wider, within the bound.
No kernel may reach another device: no remote copies, remote signals or barrier semaphores. Data moves between devices by JAX's collectives and lax.ppermute only.
A program may use at most 320 MiB of HBM per device.

v0:
```python
import jax
import jax.numpy as jnp
from jax import lax
from jax.sharding import PartitionSpec as P

epsilon = 1e-05
rope_base = 1000000.0
contract_last = (((1,), (1,)), ((), ()))
contract_first = (((0,), (0,)), ((), ()))


def rms_scale(value_heads):
    return lax.rsqrt(jnp.mean(value_heads * value_heads, axis=-1, keepdims=True) + epsilon)


def rotate(value_heads, cosines, sine_table):
    half_dim = value_heads.shape[-1] // 2
    first_half = value_heads[..., :half_dim]
    second_half = value_heads[..., half_dim:]
    return jnp.concatenate(
        [
            first_half * cosines - second_half * sine_table,
            second_half * cosines + first_half * sine_table,
        ],
        axis=-1,
    )


def unrotate(grads_in, cosines, sine_table):
    half_dim = grads_in.shape[-1] // 2
    first_half = grads_in[..., :half_dim]
    second_half = grads_in[..., half_dim:]
    return jnp.concatenate(
        [
            first_half * cosines + second_half * sine_table,
            second_half * cosines - first_half * sine_table,
        ],
        axis=-1,
    )


def angles(positions, head_dim):
    freq_index = jnp.arange(head_dim // 2, dtype=jnp.float32)
    inverse = rope_base ** (-(2.0 * freq_index) / head_dim)
    turned = positions.astype(jnp.float32)[:, None] * inverse[None, :]
    return (jnp.cos(turned)[:, None, :], jnp.sin(turned)[:, None, :])


def norm_back(grad_out, normed_hat, inv_scale, gain):
    scaled = grad_out * gain
    return inv_scale * (scaled - normed_hat * jnp.mean(scaled * normed_hat, axis=-1, keepdims=True))


def matmul(left, right):
    return jnp.dot(left, right, preferred_element_type=jnp.float32)


def matmul_t(left, right):
    return lax.dot_general(left, right, contract_last, preferred_element_type=jnp.float32)


def matmul_tn(left, right):
    return lax.dot_general(left, right, contract_first, preferred_element_type=jnp.float32)


def reduce_rows(term_fn, keep_rows):
    return lax.psum_scatter(
        term_fn(jnp.int32(0), lax.axis_size(("dp", "seq")) * keep_rows),
        ("dp", "seq"),
        scatter_dimension=0,
        tiled=True,
    )


def local(
    tokens,
    positions,
    cotangent,
    q_weight,
    key_matrix,
    value_matrix,
    out_weight,
    gate_weight,
    up_weight,
    down_weight,
    attn_gain,
    ffn_gain,
    q_gain,
    k_gain,
):
    seq_count, tok_local, model_width = tokens.shape
    rank_count = lax.axis_size("seq")
    row_count = seq_count * tok_local
    head_dim = q_gain.shape[0]
    q_cols = q_weight.shape[1]
    kv_cols = key_matrix.shape[1]
    ff_width = gate_weight.shape[1]
    local_q = q_cols // head_dim // rank_count
    local_kv = kv_cols // head_dim // rank_count
    group_size = local_q // local_kv
    sequence_length = tok_local * rank_count
    block_rows = min(512, sequence_length)
    block_count = sequence_length // block_rows
    score_scale = head_dim ** (-0.5)
    keep_rows = model_width // (lax.axis_size("dp") * rank_count)
    f32 = jnp.float32
    bf16 = jnp.bfloat16
    flat_in = tokens.reshape(row_count, model_width).astype(f32)
    in_scale = rms_scale(flat_in)
    in_hat = flat_in * in_scale
    normed_in = (in_hat * attn_gain).astype(bf16)
    q_part = lax.all_gather(q_weight, "dp", axis=0, tiled=True)
    k_part = lax.all_gather(key_matrix, "dp", axis=0, tiled=True)
    v_part = lax.all_gather(value_matrix, "dp", axis=0, tiled=True)
    out_part = lax.all_gather(out_weight, "dp", axis=0, tiled=True)
    columns = normed_in
    q_proj = matmul(columns, q_part)
    key_projected = matmul(columns, k_part)
    v_proj = matmul(columns, v_part)
    out_full = out_part
    cosines, sine_table = angles(positions.reshape(row_count), head_dim)
    q_heads = q_proj.reshape(row_count, q_cols // head_dim, head_dim)
    q_inv = rms_scale(q_heads)
    q_hat = q_heads * q_inv
    query_rows_all = rotate(q_hat * q_gain, cosines, sine_table).astype(bf16)
    key_heads = key_projected.reshape(row_count, kv_cols // head_dim, head_dim)
    k_inv = rms_scale(key_heads)
    k_hat = key_heads * k_inv
    key_rows = rotate(k_hat * k_gain, cosines, sine_table).astype(bf16)
    value_rows = v_proj.astype(bf16)
    q_send = query_rows_all.reshape(seq_count, tok_local, rank_count, local_q * head_dim)
    kv_send = jnp.concatenate(
        [
            key_rows.reshape(seq_count, tok_local, rank_count, local_kv * head_dim),
            value_rows.reshape(seq_count, tok_local, rank_count, local_kv * head_dim),
        ],
        axis=3,
    )
    q_here, kv_here = (
        lax.all_to_all(q_send, "seq", split_axis=2, concat_axis=1, tiled=True),
        lax.all_to_all(kv_send, "seq", split_axis=2, concat_axis=1, tiled=True),
    )
    q_local = q_here.reshape(seq_count, sequence_length, local_kv, group_size, head_dim)
    k_local = kv_here[:, :, 0, : local_kv * head_dim].reshape(
        seq_count, sequence_length, local_kv, head_dim
    )
    v_local = kv_here[:, :, 0, local_kv * head_dim :].reshape(
        seq_count, sequence_length, local_kv, head_dim
    )

    def block_scores(q_block, block_index):
        key_span = (block_index + 1) * block_rows
        raw_scores = (
            jnp.einsum(
                "sqhgd,skhd->shgqk", q_block, k_local[:, :key_span], preferred_element_type=f32
            )
            * score_scale
        )
        query_pos = block_index * block_rows + jnp.arange(block_rows)[:, None]
        key_pos = jnp.arange(key_span)[None, :]
        return jnp.where(key_pos <= query_pos, raw_scores, -1e30)

    attended_list = []
    log_list = []
    for block_index in range(block_count):
        row_lo = block_index * block_rows
        key_span = row_lo + block_rows
        scores = block_scores(q_local[:, row_lo : row_lo + block_rows], block_index)
        row_max = jnp.max(scores, axis=-1, keepdims=True)
        exp_terms = jnp.exp(scores - row_max)
        summed = jnp.sum(exp_terms, axis=-1, keepdims=True)
        probs = exp_terms / summed
        log_list.append(row_max + jnp.log(summed))
        attended_list.append(
            jnp.einsum(
                "shgqk,skhd->sqhgd",
                probs.astype(bf16),
                v_local[:, :key_span],
                preferred_element_type=f32,
            )
        )
    attended_output = jnp.concatenate(attended_list, axis=1)
    log_total = jnp.concatenate(log_list, axis=3)
    mixed_send = attended_output.astype(bf16).reshape(
        seq_count, sequence_length, 1, local_q * head_dim
    )
    mixed_back = lax.all_to_all(mixed_send, "seq", split_axis=1, concat_axis=2, tiled=True)
    mixed_rows = mixed_back.reshape(row_count, q_cols)
    residual = flat_in + matmul_t(mixed_rows, out_full)
    mid_scale = rms_scale(residual)
    mid_hat = residual * mid_scale
    normed_mid = (mid_hat * ffn_gain).astype(bf16)
    gate_part = lax.all_gather(gate_weight, "dp", axis=0, tiled=True)
    up_part = lax.all_gather(up_weight, "dp", axis=0, tiled=True)
    columns = normed_mid
    gate_proj = matmul(columns, gate_part)
    up_proj = matmul(columns, up_part)
    sigmoid_gate = jax.nn.sigmoid(gate_proj)
    activated = gate_proj * sigmoid_gate
    hidden = (activated * up_proj).astype(bf16)
    ffn_branch = matmul_t(hidden, lax.all_gather(down_weight, "dp", axis=0, tiled=True))
    output = (residual + ffn_branch).astype(bf16).reshape(seq_count, tok_local, model_width)
    d_ffn = cotangent.reshape(row_count, model_width)
    columns = d_ffn
    d_hidden = matmul(columns, lax.all_gather(down_weight, "dp", axis=0, tiled=True))
    d_gate = (d_hidden * up_proj * sigmoid_gate * (1.0 + gate_proj * (1.0 - sigmoid_gate))).astype(
        bf16
    )
    d_up = (d_hidden * activated).astype(bf16)
    gate_part, up_part = lax.all_gather((gate_weight, up_weight), "dp", axis=0, tiled=True)
    d_mid = matmul_t(d_gate, gate_part) + matmul_t(d_up, up_part)
    ffn_gain_part = jnp.sum(d_mid * mid_hat, axis=0)
    d_resid = d_ffn.astype(f32) + norm_back(d_mid, mid_hat, mid_scale, ffn_gain)
    d_attn = d_resid.astype(bf16)
    d_mixed = matmul(d_attn, out_full).astype(bf16)
    d_mixed_send = d_mixed.reshape(seq_count, tok_local, rank_count, local_q * head_dim)
    d_mixed_here = lax.all_to_all(d_mixed_send, "seq", split_axis=2, concat_axis=1, tiled=True)
    d_mixed_local = d_mixed_here.reshape(seq_count, sequence_length, local_kv, group_size, head_dim)
    d_key = jnp.zeros((seq_count, sequence_length, local_kv, head_dim), f32)
    d_value = jnp.zeros((seq_count, sequence_length, local_kv, head_dim), f32)
    d_query_list = []
    for block_index in range(block_count):
        row_lo = block_index * block_rows
        key_span = row_lo + block_rows
        q_block = q_local[:, row_lo : row_lo + block_rows]
        grad_block = d_mixed_local[:, row_lo : row_lo + block_rows]
        probs = jnp.exp(
            block_scores(q_block, block_index) - log_total[:, :, :, row_lo : row_lo + block_rows]
        )
        d_value = d_value.at[:, :key_span].add(
            jnp.einsum(
                "shgqk,sqhgd->skhd", probs.astype(bf16), grad_block, preferred_element_type=f32
            )
        )
        d_weights = jnp.einsum(
            "sqhgd,skhd->shgqk", grad_block, v_local[:, :key_span], preferred_element_type=f32
        )
        delta = jnp.sum(
            grad_block.astype(f32) * attended_output[:, row_lo : row_lo + block_rows], axis=-1
        )
        delta = jnp.transpose(delta, (0, 2, 3, 1))[..., None]
        d_scores = (probs * (d_weights - delta)).astype(bf16)
        d_query_list.append(
            jnp.einsum(
                "shgqk,skhd->sqhgd", d_scores, k_local[:, :key_span], preferred_element_type=f32
            )
            * score_scale
        )
        d_key = d_key.at[:, :key_span].add(
            jnp.einsum("shgqk,sqhgd->skhd", d_scores, q_block, preferred_element_type=f32)
            * score_scale
        )
    d_query = (
        jnp.concatenate(d_query_list, axis=1)
        .astype(bf16)
        .reshape(seq_count, sequence_length, 1, local_q * head_dim)
    )
    d_kv = jnp.concatenate(
        [
            d_key.astype(bf16).reshape(seq_count, sequence_length, 1, local_kv * head_dim),
            d_value.astype(bf16).reshape(seq_count, sequence_length, 1, local_kv * head_dim),
        ],
        axis=3,
    )
    d_query_rows, d_kv_rows = (
        lax.all_to_all(d_query, "seq", split_axis=1, concat_axis=2, tiled=True),
        lax.all_to_all(d_kv, "seq", split_axis=1, concat_axis=2, tiled=True),
    )
    d_q_rot = d_query_rows.reshape(row_count, q_cols // head_dim, head_dim).astype(f32)
    d_k_rot = (
        d_kv_rows[..., : local_kv * head_dim]
        .reshape(row_count, kv_cols // head_dim, head_dim)
        .astype(f32)
    )
    d_v_proj = d_kv_rows[..., local_kv * head_dim :].reshape(row_count, kv_cols)
    d_q_normed = unrotate(d_q_rot, cosines, sine_table)
    d_k_normed = unrotate(d_k_rot, cosines, sine_table)
    q_gain_part = jnp.sum(d_q_normed * q_hat, axis=(0, 1))
    k_gain_part = jnp.sum(d_k_normed * k_hat, axis=(0, 1))
    d_q_proj = norm_back(d_q_normed, q_hat, q_inv, q_gain).reshape(row_count, q_cols).astype(bf16)
    d_k_proj = norm_back(d_k_normed, k_hat, k_inv, k_gain).reshape(row_count, kv_cols).astype(bf16)
    q_part, k_part, v_part = lax.all_gather(
        (q_weight, key_matrix, value_matrix), "dp", axis=0, tiled=True
    )
    d_normed_in = (
        matmul_t(d_q_proj, q_part) + matmul_t(d_k_proj, k_part) + matmul_t(d_v_proj, v_part)
    )
    attn_gain_part = jnp.sum(d_normed_in * in_hat, axis=0)
    input_grad = (
        (d_resid + norm_back(d_normed_in, in_hat, in_scale, attn_gain))
        .astype(bf16)
        .reshape(seq_count, tok_local, model_width)
    )

    def every_term(offset, amount):
        return jnp.concatenate(
            [
                jnp.concatenate(
                    [
                        matmul_tn(normed_mid, d_gate),
                        matmul_tn(normed_mid, d_up),
                        matmul_tn(d_ffn, hidden),
                    ],
                    axis=1,
                ),
                matmul_tn(d_attn, mixed_rows),
                jnp.concatenate(
                    [
                        matmul_tn(normed_in, d_q_proj),
                        matmul_tn(normed_in, d_k_proj),
                        matmul_tn(normed_in, d_v_proj),
                    ],
                    axis=1,
                ),
            ],
            axis=1,
        )

    combined = reduce_rows(every_term, keep_rows)
    ffn_part = combined[:, : 3 * ff_width]
    out_part = combined[:, 3 * ff_width : 3 * ff_width + q_cols]
    first_part = combined[:, 3 * ff_width + q_cols :]
    ffn_full, out_grad, first_full = (
        lax.all_gather(ffn_part.astype(jnp.bfloat16), "seq", axis=0, tiled=True).astype(
            ffn_part.dtype
        ),
        lax.all_gather(out_part.astype(jnp.bfloat16), "seq", axis=0, tiled=True).astype(
            out_part.dtype
        ),
        lax.all_gather(first_part.astype(jnp.bfloat16), "seq", axis=0, tiled=True).astype(
            first_part.dtype
        ),
    )
    gain_grads = lax.psum((attn_gain_part, ffn_gain_part, q_gain_part, k_gain_part), ("dp", "seq"))
    return (
        output,
        input_grad,
        first_full[:, :q_cols],
        first_full[:, q_cols : q_cols + kv_cols],
        first_full[:, q_cols + kv_cols :],
        out_grad,
        ffn_full[:, :ff_width],
        ffn_full[:, ff_width : 2 * ff_width],
        ffn_full[:, 2 * ff_width :],
        gain_grads[0],
        gain_grads[1],
        gain_grads[2],
        gain_grads[3],
    )


def solution(mesh):
    in_specs = (
        P("dp", "seq", None),
        P("dp", "seq"),
        P("dp", "seq", None),
        P("dp", None),
        P("dp", None),
        P("dp", None),
        P("dp", None),
        P("dp", None),
        P("dp", None),
        P("dp", None),
        P(),
        P(),
        P(),
        P(),
    )
    out_specs = (
        P("dp", "seq", None),
        P("dp", "seq", None),
        P("dp", None),
        P("dp", None),
        P("dp", None),
        P("dp", None),
        P("dp", None),
        P("dp", None),
        P("dp", None),
        P(),
        P(),
        P(),
        P(),
    )
    return jax.shard_map(local, mesh=mesh, in_specs=in_specs, out_specs=out_specs, check_vma=False)
```

profile of v0, /device:TPU:0, one launch (start us, length us, event | category | flops | bytes accessed | tf_op | source)
XLA Modules:
  0.0 1240.2 jit_solution(9845809243946968209)
XLA Ops:
  13.9 22.2 %all-gather.11.cloned.1.call-done = bf16[1024,512]{1,0:T(8,128)(2,1)} async-done(((bf16[128,512]{1,0:T(8,128)(2,1)}), bf16[1024,512]{1,0:T(8,128)(2,1)}) %all-gather.11.cloned.1.call-update) | async-done | bytes 1048592 | tf_op jit(solution)/shard_map/all_gather | solution.py:114
  40.9 20.6 %all-gather.9.cloned.1.call-done = bf16[1024,512]{1,0:T(8,128)(2,1)} async-done(((bf16[128,512]{1,0:T(8,128)(2,1)}), bf16[1024,512]{1,0:T(8,128)(2,1)}) %all-gather.9.cloned.1.call-update) | async-done | bytes 1048592 | tf_op jit(solution)/shard_map/all_gather | solution.py:113
  68.0 4.6 all-to-all-start
  72.6 18.8 %all-gather.13.cloned.1.call-done = bf16[1024,1024]{1,0:T(8,128)(2,1)} async-done(((bf16[128,1024]{1,0:T(8,128)(2,1)}), bf16[1024,1024]{1,0:T(8,128)(2,1)}) %all-gather.13.cloned.1.call-update) | async-done | bytes 2097168 | tf_op jit(solution)/shard_map/all_gather | solution.py:112
  91.4 3.9 copy.109
  101.6 4.8 all-to-all-start.1
  109.9 22.6 %all-to-all-done.1 = bf16[2,256,4,256]{1,0,3,2:T(2,128)(2,1)S(1)} async-done(((bf16[2,256,4,256]{1,0,3,2:T(2,128)(2,1)}), bf16[2,256,4,256]{1,0,3,2:T(2,128)(2,1)S(1)}, u32[]{:S(2)}, u32[]{:S(2)}) %all-to-all-start.1) | async-done | bytes 1048608 | tf_op jit(solution)/shard_map/all_to_all | solution.py:140
  138.6 3.3 fusion.85
  143.9 7.5 fusion.5
  151.5 10.7 fusion.2
  162.2 9.4 fusion.84
  174.4 3.9 all-to-all-start.2
  178.3 25.2 %all-to-all-done.2 = bf16[2,1024,1,256]{3,0,2,1:T(2,128)(2,1)S(1)} async-done(((bf16[2,1024,1,256]{3,0,2,1:T(2,128)(2,1)}), bf16[2,1024,1,256]{3,0,2,1:T(2,128)(2,1)S(1)}, u32[]{:S(2)}, u32[]{:S(2)}) %all-to-all-start.2) | async-done | bytes 1048608 | tf_op jit(solution)/shard_map/all_to_all | solution.py:187
  205.8 3.3 multiply_reduce_fusion.4
  209.4 12.1 fusion.87
  221.4 20.8 %all-gather.17.cloned.1.call-done = bf16[1024,4608]{1,0:T(8,128)(2,1)} async-done(((bf16[128,4608]{1,0:T(8,128)(2,1)}), bf16[1024,4608]{1,0:T(8,128)(2,1)}) %all-gather.17.cloned.1.call-update) | async-done | bytes 9437200 | tf_op jit(solution)/shard_map/all_gather | solution.py:193
  242.3 11.0 fusion.86
  253.3 49.7 %all-gather.21.cloned.1.call-done = bf16[1024,4608]{1,0:T(8,128)(2,1)} async-done(((bf16[128,4608]{1,0:T(8,128)(2,1)}), bf16[1024,4608]{1,0:T(8,128)(2,1)}) %all-gather.21.cloned.1.call-update) | async-done | bytes 9437200 | tf_op jit(solution)/shard_map/all_gather | solution.py:201
  303.0 17.6 %multiply_convert_fusion = (bf16[512,4608]{1,0:T(8,128)(2,1)}, bf16[512,4608]{1,0:T(8,128)(2,1)}, bf16[512,4608]{1,0:T(8,128)(2,1)}) fusion(f32[512,4608]{1,0:T(8,128)} %fusion.86, f32[512,4608]{1,0:T(8,128)} %fusion.87, bf16[512,1024]{1,0:T(8,128)(2,1)} %bitcast.306, bf16[1024,4608]{1,0:T(8,128)(2,1)} %all-gather.21.cloned.1.call-done), kind=kOutput, calls=%fused_computation.12 | convolution fusion | flops 4867227648 | bytes 43515904 | tf_op jit(solution)/shard_map/dot_general | solution.py:55
  320.6 9.2 fusion.88
  329.8 8.1 multiply_reduce_fusion.1
  347.6 4.8 all-to-all-start.3
  352.4 11.8 convolution_dynamic-update-slice_fusion.1
  364.1 11.6 convolution_dynamic-update-slice_fusion
  383.5 5.9 fusion.50
  389.9 6.4 fusion.7
  396.3 8.9 fusion.44
  405.1 11.2 fusion.1
  418.3 3.6 fusion.54
  421.9 6.8 fusion.47
  430.0 3.1 pad_maximum_fusion.5
  433.2 4.2 all-to-all-start.5
  437.4 11.8 bitcast_dynamic-update-slice_fusion
  449.3 4.9 fusion.49
  455.3 4.0 fusion.48
  461.2 3.5 pad_maximum_fusion.4
  464.8 5.0 all-to-all-start.4
  470.2 3.4 convolution_dynamic-update-slice_fusion.3
  485.6 9.0 all-to-all-done.4
  497.5 4.2 copy.124
  501.7 3.9 reshape.510
  509.4 3.4 convolution_dynamic-update-slice_fusion.2
  517.4 612.6 %reduce-scatter.2.cloned.1.call-done = f32[32,16896]{1,0:T(8,128)} async-done(((f32[1024,16896]{1,0:T(8,128)}), f32[32,16896]{1,0:T(8,128)}) %reduce-scatter.2.cloned.1.call-update) | async-done | bytes 2162704 | tf_op jit(solution)/shard_map/reduce_scatter | solution.py:67
  1133.7 10.3 add_convert_fusion
  1148.9 42.6 %all-reduce.2 = (f32[1024]{0:T(1024)}, f32[1024]{0:T(1024)}, f32[64]{0:T(128)}, f32[64]{0:T(128)}) all-reduce(f32[1024]{0:T(1024)S(1)} %get-tuple-element.81, f32[1024]{0:T(1024)S(1)} %get-tuple-element.79, f32[64]{0:T(128)S(1)} %get-tuple-element.77, f32[64]{0:T(128)S(1)} %get-tuple-element.83), channel_id=1, replica_groups=mesh['dp'=8,'seq'=4] {'dp','seq'}, use_global_device_ids=true, to_apply=%region_16.17 | all-reduce | flops 2176 | bytes 17408 | tf_op jit(solution)/shard_map/psum | solution.py:334
  1194.7 15.7 %all_gather.44 = bf16[128,1024]{1,0:T(8,128)(2,1)S(1)} all-gather(bf16[32,1024]{1,0:T(8,128)(2,1)S(1)} %slice-done), channel_id=1, replica_groups=mesh['dp'=8,'seq'=4] {'seq'}, dimensions={0}, use_global_device_ids=true | all-gather | bytes 327680 | tf_op jit(solution)/shard_map/all_gather | solution.py:327
  1211.2 15.4 %all_gather.43 = bf16[128,2048]{1,0:T(8,128)(2,1)S(1)} all-gather(bf16[32,2048]{1,0:T(8,128)(2,1)S(1)} %slice-done.1), channel_id=1, replica_groups=mesh['dp'=8,'seq'=4] {'seq'}, dimensions={0}, use_global_device_ids=true | all-gather | bytes 655360 | tf_op jit(solution)/shard_map/all_gather | solution.py:330
  1228.3 5.2 fusion.80
  (221 shorter events, 102.5 us)
Async XLA Ops:
  7.2 5.7 copy-start.43
  7.2 28.9 %all-gather.11.cloned.1.call-start = ((), (), s32[]{:S(2)}) async-start(), calls=%async_computation.8 | async-start | bytes 1179648 | tf_op jit(solution)/shard_map/all_gather | solution.py:114
  7.9 53.6 %all-gather.9.cloned.1.call-start = ((), (), s32[]{:S(2)}) async-start(), calls=%async_computation.7 | async-start | bytes 1179648 | tf_op jit(solution)/shard_map/all_gather | solution.py:113
  8.7 82.7 %all-gather.13.cloned.1.call-start = ((), (), s32[]{:S(2)}) async-start(), calls=%async_computation.9 | async-start | bytes 2359296 | tf_op jit(solution)/shard_map/all_gather | solution.py:112
  9.4 196.3 %all-gather.15.cloned.1.call-start = ((), (), s32[]{:S(2)}) async-start(), calls=%async_computation.10 | async-start | bytes 2359296 | tf_op jit(solution)/shard_map/all_gather | solution.py:115
  10.0 199.4 %all-gather.19.cloned.1.call-start = ((), (), s32[]{:S(2)}) async-start(), calls=%async_computation.12 | async-start | bytes 10616832 | tf_op jit(solution)/shard_map/all_gather | solution.py:194
  10.6 231.7 %all-gather.17.cloned.1.call-start = ((), (), s32[]{:S(2)}) async-start(), calls=%async_computation.11 | async-start | bytes 10616832 | tf_op jit(solution)/shard_map/all_gather | solution.py:193
  11.2 291.8 %all-gather.21.cloned.1.call-start = ((), (), s32[]{:S(2)}) async-start(), calls=%async_computation.13 | async-start | bytes 10616832 | tf_op jit(solution)/shard_map/all_gather | solution.py:201
  13.3 82.1 %copy-start.11 = (bf16[2,256,1024]{2,1,0:T(8,128)(2,1)}, bf16[2,256,1024]{2,1,0:T(8,128)(2,1)S(1)}, u32[]{:S(2)}) copy-start(bf16[2,256,1024]{2,1,0:T(8,128)(2,1)S(1)} %fusion.32) | copy-start | bytes 3145732
  13.9 86.1 %copy-start.26 = (f32[512,32]{0,1:T(8,128)}, f32[512,32]{0,1:T(8,128)S(1)}, u32[]{:S(2)}) copy-start(f32[512,32]{0,1:T(8,128)S(1)} %get-tuple-element.111) | copy-start | bytes 196612
  13.9 86.1 %copy-start.28 = (f32[512,32]{0,1:T(8,128)}, f32[512,32]{0,1:T(8,128)S(1)}, u32[]{:S(2)}) copy-start(f32[512,32]{0,1:T(8,128)S(1)} %get-tuple-element.112) | copy-start | bytes 196612
  38.9 25.9 %copy-start.50 = (f32[64]{0:T(128)S(1)}, f32[64]{0:T(128)}, u32[]{:S(2)}) copy-start(f32[64]{0:T(128)} %param.39) | copy-start | bytes 772
  68.0 33.6 %all-to-all-start = ((bf16[2,256,4,256]{3,1,0,2:T(8,128)(2,1)}), bf16[2,256,4,256]{3,1,0,2:T(8,128)(2,1)S(1)}, u32[]{:S(2)}, u32[]{:S(2)}) async-start(bf16[2,256,4,256]{3,1,0,2:T(8,128)(2,1)} %pad_maximum_fusion.1), calls=%async_computation | async-start | bytes 2097152 | tf_op jit(solution)/shard_map/all_to_all | solution.py:141
  91.4 8.2 copy-start.48
  101.6 30.9 %all-to-all-start.1 = ((bf16[2,256,4,256]{1,0,3,2:T(2,128)(2,1)}), bf16[2,256,4,256]{1,0,3,2:T(2,128)(2,1)S(1)}, u32[]{:S(2)}, u32[]{:S(2)}) async-start(bf16[2,256,4,256]{1,0,3,2:T(2,128)(2,1)} %convert_element_type.176), calls=%async_computation.1 | async-start | bytes 2097152 | tf_op jit(solution)/shard_map/all_to_all | solution.py:140
  134.1 9.8 copy-start.14
  151.4 10.7 copy-start.39
  162.2 9.8 copy-start.25
  174.4 29.2 %all-to-all-start.2 = ((bf16[2,1024,1,256]{3,0,2,1:T(2,128)(2,1)}), bf16[2,1024,1,256]{3,0,2,1:T(2,128)(2,1)S(1)}, u32[]{:S(2)}, u32[]{:S(2)}) async-start(bf16[2,1024,1,256]{3,0,2,1:T(2,128)(2,1)} %pad_maximum_fusion.3), calls=%async_computation.2 | async-start | bytes 2097152 | tf_op jit(solution)/shard_map/all_to_all | solution.py:187
  209.1 120.7 %copy-start.7 = (f32[512,1024]{1,0:T(8,128)}, f32[512,1024]{1,0:T(8,128)S(1)}, u32[]{:S(2)}) copy-start(f32[512,1024]{1,0:T(8,128)S(1)} %get-tuple-element.128) | copy-start | bytes 6291460
  320.6 9.2 copy-start.9
  329.8 8.1 copy-start.33
  347.6 31.0 %all-to-all-start.3 = ((bf16[2,256,4,256]{1,3,0,2:T(8,128)(2,1)}), bf16[2,256,4,256]{1,3,0,2:T(8,128)(2,1)}, u32[]{:S(2)}, u32[]{:S(2)}) async-start(bf16[2,256,4,256]{1,3,0,2:T(8,128)(2,1)} %copy.117), calls=%async_computation.3 | async-start | bytes 2097152 | tf_op jit(solution)/shard_map/all_to_all | solution.py:217
  383.4 12.9 %copy-start.17 = (bf16[2,1024,2,2,64]{1,4,3,2,0:T(8,128)(2,1)}, bf16[2,1024,2,2,64]{1,4,3,2,0:T(8,128)(2,1)S(1)}, u32[]{:S(2)}) copy-start(bf16[2,1024,2,2,64]{1,4,3,2,0:T(8,128)(2,1)S(1)} %reshape.504) | copy-start | bytes 3145732
  383.4 6.0 copy-start.31
  383.4 6.0 copy-start.32
  383.4 6.4 copy-start.40
  389.9 6.4 copy-start.21
  405.1 13.2 %copy-start.15 = (bf16[2,1024,2,2,64]{1,4,3,2,0:T(8,128)(2,1)S(1)}, bf16[2,1024,2,2,64]{1,4,3,2,0:T(8,128)(2,1)}, u32[]{:S(2)}) copy-start(bf16[2,1024,2,2,64]{1,4,3,2,0:T(8,128)(2,1)} %copy-done.14) | copy-start | bytes 3145732
  433.2 31.6 %all-to-all-start.5 = ((bf16[2,1024,1,256]{3,0,2,1:T(2,128)(2,1)}), bf16[2,1024,1,256]{3,0,2,1:T(2,128)(2,1)}, u32[]{:S(2)}, u32[]{:S(2)}) async-start(bf16[2,1024,1,256]{3,0,2,1:T(2,128)(2,1)} %pad_maximum_fusion.5), calls=%async_computation.5 | async-start | bytes 2097152 | tf_op jit(solution)/shard_map/all_to_all | solution.py:267
  437.4 11.9 copy-start.19
  455.3 14.9 %copy-start.16 = (bf16[64,8,4,256]{3,1,2,0:T(8,128)(2,1)S(1)}, bf16[64,8,4,256]{3,1,2,0:T(8,128)(2,1)}, u32[]{:S(2)}) copy-start(bf16[64,8,4,256]{3,1,2,0:T(8,128)(2,1)} %copy.162) | copy-start | bytes 3145732
  464.8 29.9 %all-to-all-start.4 = ((bf16[2,1024,1,256]{3,0,2,1:T(2,128)(2,1)}), bf16[2,1024,1,256]{3,0,2,1:T(2,128)(2,1)}, u32[]{:S(2)}, u32[]{:S(2)}) async-start(bf16[2,1024,1,256]{3,0,2,1:T(2,128)(2,1)} %pad_maximum_fusion.4), calls=%async_computation.4 | async-start | bytes 2097152 | tf_op jit(solution)/shard_map/all_to_all | solution.py:266
  469.8 660.2 %reduce-scatter.2.cloned.1.call-start = ((), (), s32[]{:S(2)}) async-start(), calls=%async_computation.14 | async-start | bytes 71368704 | tf_op jit(solution)/shard_map/reduce_scatter | solution.py:67
  473.7 9.1 copy-start.27
  473.7 9.1 copy-start.29
  475.1 9.0 copy-start.5
  475.1 9.0 copy-start.42
  475.1 9.0 copy-start.51
  501.7 5.9 copy-start.37
  501.7 5.9 copy-start.49
  509.4 5.7 copy-start.34
  517.2 711.1 %all-gather.23.cloned.1.call-start = ((), (), s32[]{:S(2)}) async-start(), calls=%async_computation.15 | async-start | bytes 4423680 | tf_op jit(solution)/shard_map/all_gather | solution.py:324
  1133.7 10.3 copy-start.13
  1133.7 11.1 copy-start.24
  1133.7 11.1 copy-start.35
  1148.9 45.7 %slice-start = ((bf16[32,16896]{1,0:T(8,128)(2,1)}), bf16[32,1024]{1,0:T(8,128)(2,1)S(1)}, s32[]{:S(2)}) async-start(bf16[32,16896]{1,0:T(8,128)(2,1)} %copy-done.10), calls=%async_computation.16 | async-start | bytes 131072 | tf_op jit(solution)/shard_map/slice | solution.py:321
  1148.9 62.3 %slice-start.1 = ((bf16[32,16896]{1,0:T(8,128)(2,1)}), bf16[32,2048]{1,0:T(8,128)(2,1)S(1)}, s32[]{:S(2)}) async-start(bf16[32,16896]{1,0:T(8,128)(2,1)} %copy-done.10), calls=%async_computation.17 | async-start | bytes 262144 | tf_op jit(solution)/shard_map/slice | solution.py:322
  (22 other events, 56.8 us)
Sparse Core Ops, SparseCore 0:
  9.9 26.1 all-gather.10
  38.0 23.4 all-gather.8
  63.5 27.8 all-gather.12
  93.1 27.8 all-gather.14
  122.8 58.8 all-gather.18
  183.4 58.8 all-gather.16
  244.1 58.8 all-gather.20
  517.3 612.6 reduce-scatter.1
  1133.8 73.3 all-gather.22
where the time goes:
time: 1250 us; the launch traced here: 1240 us
  waiting for transfers between devices  809 us (65%)
  matrix products  206 us (16%)
  blocking collectives  73.7 us (6%)
  local copies, waits for them, and re-layouts  63 us (5%)
  other arithmetic  45.8 us (4%)
  starting transfers between devices  28.2 us (2%)
  between operations  15 us (1%)
    reduce_scatter x1, waiting for transfers between devices, reduce_rows(): lax.psum_scatter(term_fn(jnp.int32(0), lax.axis_size(('dp', 'seq')) * kee...  613 us
    all_gather x1, waiting for transfers between devices, local(): lax.all_gather(down_weight, 'dp', axis=0, tiled=True)  49.7 us
    dot_general x7, matrix products, matmul(): return jnp.dot(left, right, preferred_element_type=jnp.float32)  49.3 us
    dot_general x7, matrix products, matmul_tn(): lax.dot_general(left, right, contract_first, preferred_element_type=jnp.f...  46.4 us
    psum x1, blocking collectives, local(): lax.psum((attn_gain_part, ffn_gain_part, q_gain_part, k_gain_part), ('dp'...  42.6 us
    dot_general x7, matrix products, matmul_t(): lax.dot_general(left, right, contract_last, preferred_element_type=jnp.fl...  35.4 us
    all_to_all x1, waiting for transfers between devices, local(): lax.all_to_all(mixed_send, 'seq', split_axis=1, concat_axis=2, tiled=True)  25.2 us
  transfers between devices with their start and end apart: 15, of which 10 were waited for; matrix products, arithmetic and copies ran while one was open for 15% of the time, Pallas kernels for 0%

commit v1 on v0

--- a/solution.py
+++ b/solution.py
@@ -7,6 +7,19 @@
 rope_base = 1000000.0
 contract_last = (((1,), (1,)), ((), ()))
 contract_first = (((0,), (0,)), ((), ()))
+
+
+def gather_around(x, axis, dim):
+    ways = lax.axis_size(axis)
+    up = [(d, (d + 1) % ways) for d in range(ways)]
+    down = [(d, (d - 1) % ways) for d in range(ways)]
+    earlier, later = ([x], [x])
+    for _ in range(ways // 2):
+        earlier.append(lax.ppermute(earlier[-1], axis, up))
+    for _ in range((ways - 1) // 2):
+        later.append(lax.ppermute(later[-1], axis, down))
+    line = jnp.concatenate([*earlier[::-1], *later[1:]], axis=dim)
+    return jnp.roll(line, (lax.axis_index(axis) - ways // 2) * x.shape[dim], axis=dim)
 
 
 def rms_scale(value_heads):
@@ -198,7 +211,7 @@
     sigmoid_gate = jax.nn.sigmoid(gate_proj)
     activated = gate_proj * sigmoid_gate
     hidden = (activated * up_proj).astype(bf16)
-    ffn_branch = matmul_t(hidden, lax.all_gather(down_weight, "dp", axis=0, tiled=True))
+    ffn_branch = matmul_t(hidden, gather_around(down_weight, "dp", 0))
     output = (residual + ffn_branch).astype(bf16).reshape(seq_count, tok_local, model_width)
     d_ffn = cotangent.reshape(row_count, model_width)
     columns = d_ffn

time: 1250 us -> 1260 us (level)
  waiting for transfers between devices: 809 us -> 771 us
  local copies, waits for them, and re-layouts: 63 us -> 94.5 us
  starting transfers between devices: 28.2 us -> 47 us
    reduce_scatter x1, waiting for transfers between devices: 613 us -> 489 us  [reduce_rows(): lax.psum_scatter(term_fn(jnp.int32(0), lax.axis_size(('dp', 'seq')) * kee...]
    ppermute x0 -> x7, waiting for transfers between devices: none -> 95.1 us  [the longest x4 95.1 us: gather_around(): earlier.append(lax.ppermute(earlier[-1], axis, up))]
    unnamed x109 -> x146, local copies, waits for them, and re-layouts: 5.2 us -> 35.6 us
  transfers between devices with their start and end apart: 15 -> 22, of which waited for: 10 -> 14; matrix products, arithmetic and copies ran while one was open for 15% -> 17% of each run, Pallas kernels for 0% -> 0%
where the time goes in v1:
time: 1260 us; the launch traced here: 1250 us
  waiting for transfers between devices  771 us (61%)
  matrix products  206 us (16%)
  local copies, waits for them, and re-layouts  94.5 us (8%)
  blocking collectives  73.2 us (6%)
  starting transfers between devices  47 us (4%)
  other arithmetic  43.9 us (3%)
  between operations  15.3 us (1%)
    reduce_scatter x1, waiting for transfers between devices, reduce_rows(): lax.psum_scatter(term_fn(jnp.int32(0), lax.axis_size(('dp', 'seq')) * kee...  489 us
    ppermute x4, waiting for transfers between devices, gather_around(): earlier.append(lax.ppermute(earlier[-1], axis, up))  95.1 us
    all_gather x1, waiting for transfers between devices, local(): lax.all_gather(down_weight, 'dp', axis=0, tiled=True)  49.6 us
    dot_general x7, matrix products, matmul(): return jnp.dot(left, right, preferred_element_type=jnp.float32)  47.9 us
    dot_general x7, matrix products, matmul_tn(): lax.dot_general(left, right, contract_first, preferred_element_type=jnp.f...  46.4 us
    psum x1, blocking collectives, local(): lax.psum((attn_gain_part, ffn_gain_part, q_gain_part, k_gain_part), ('dp'...  44 us
    dot_general x7, matrix products, matmul_t(): lax.dot_general(left, right, contract_last, preferred_element_type=jnp.fl...  37.1 us
    unnamed x146, local copies, waits for them, and re-layouts  35.6 us
  transfers between devices with their start and end apart: 22, of which 14 were waited for; matrix products, arithmetic and copies ran while one was open for 17% of the time, Pallas kernels for 0%

profile of v1, /device:TPU:0, one launch (start us, length us, event | category | flops | bytes accessed | tf_op | source)
XLA Modules:
  0.0 1250.4 jit_solution(2866516812777532229)
XLA Ops:
  13.9 22.2 %all-gather.11.cloned.1.call-done = bf16[1024,512]{1,0:T(8,128)(2,1)} async-done(((bf16[128,512]{1,0:T(8,128)(2,1)}), bf16[1024,512]{1,0:T(8,128)(2,1)}) %all-gather.11.cloned.1.call-update) | async-done | bytes 1048592 | tf_op jit(solution)/shard_map/all_gather | solution.py:127
  40.9 20.6 %all-gather.9.cloned.1.call-done = bf16[1024,512]{1,0:T(8,128)(2,1)} async-done(((bf16[128,512]{1,0:T(8,128)(2,1)}), bf16[1024,512]{1,0:T(8,128)(2,1)}) %all-gather.9.cloned.1.call-update) | async-done | bytes 1048592 | tf_op jit(solution)/shard_map/all_gather | solution.py:126
  68.0 4.6 all-to-all-start
  72.6 18.8 %all-gather.13.cloned.1.call-done = bf16[1024,1024]{1,0:T(8,128)(2,1)} async-done(((bf16[128,1024]{1,0:T(8,128)(2,1)}), bf16[1024,1024]{1,0:T(8,128)(2,1)}) %all-gather.13.cloned.1.call-update) | async-done | bytes 2097168 | tf_op jit(solution)/shard_map/all_gather | solution.py:125
  91.4 3.9 copy.109
  101.6 4.8 all-to-all-start.1
  110.0 22.6 %all-to-all-done.1 = bf16[2,256,4,256]{1,0,3,2:T(2,128)(2,1)S(1)} async-done(((bf16[2,256,4,256]{1,0,3,2:T(2,128)(2,1)}), bf16[2,256,4,256]{1,0,3,2:T(2,128)(2,1)S(1)}, u32[]{:S(2)}, u32[]{:S(2)}) %all-to-all-start.1) | async-done | bytes 1048608 | tf_op jit(solution)/shard_map/all_to_all | solution.py:153
  143.9 7.6 fusion.7
  151.6 10.6 fusion.2
  162.2 9.4 fusion.89
  174.4 14.6 %all-to-all-start.2 = ((bf16[2,1024,1,256]{3,0,2,1:T(2,128)(2,1)}), bf16[2,1024,1,256]{3,0,2,1:T(2,128)(2,1)S(1)}, u32[]{:S(2)}, u32[]{:S(2)}) async-start(bf16[2,1024,1,256]{3,0,2,1:T(2,128)(2,1)} %pad_maximum_fusion.3), calls=%async_computation.2 | async-start | bytes 2097152 | tf_op jit(solution)/shard_map/all_to_all | solution.py:200
  189.0 25.1 %all-to-all-done.2 = bf16[2,1024,1,256]{3,0,2,1:T(2,128)(2,1)S(1)} async-done(((bf16[2,1024,1,256]{3,0,2,1:T(2,128)(2,1)}), bf16[2,1024,1,256]{3,0,2,1:T(2,128)(2,1)S(1)}, u32[]{:S(2)}, u32[]{:S(2)}) %all-to-all-start.2) | async-done | bytes 1048608 | tf_op jit(solution)/shard_map/all_to_all | solution.py:200
  220.4 11.3 fusion.92
  231.7 10.6 all-gather.17.cloned.1.call-done
  242.2 11.1 fusion.91
  253.4 49.6 %all-gather.21.cloned.1.call-done = bf16[1024,4608]{1,0:T(8,128)(2,1)} async-done(((bf16[128,4608]{1,0:T(8,128)(2,1)}), bf16[1024,4608]{1,0:T(8,128)(2,1)}) %all-gather.21.cloned.1.call-update) | async-done | bytes 9437200 | tf_op jit(solution)/shard_map/all_gather | solution.py:218
  303.0 16.8 %multiply_convert_fusion = (bf16[512,4608]{1,0:T(8,128)(2,1)S(1)}, bf16[512,4608]{1,0:T(8,128)(2,1)}, bf16[512,4608]{1,0:T(8,128)(2,1)}) fusion(f32[512,4608]{1,0:T(8,128)} %fusion.91, f32[512,4608]{1,0:T(8,128)} %fusion.92, bf16[512,1024]{1,0:T(8,128)(2,1)} %bitcast.305, bf16[1024,4608]{1,0:T(8,128)(2,1)} %all-gather.21.cloned.1.call-done), kind=kOutput, calls=%fused_computation.12 | convolution fusion | flops 4867227648 | bytes 43515904 | tf_op jit(solution)/shard_map/dot_general | solution.py:68
  319.8 10.8 fusion.93
  330.7 8.1 multiply_reduce_fusion.1
  347.6 5.0 all-to-all-start.3
  352.7 11.6 convolution_dynamic-update-slice_fusion.1
  364.3 11.7 convolution_dynamic-update-slice_fusion
  383.7 5.9 fusion.54
  390.2 6.4 fusion.9
  396.5 8.9 fusion.48
  405.4 11.2 fusion.1
  418.6 3.6 fusion.58
  422.1 6.8 fusion.51
  433.4 4.2 all-to-all-start.5
  437.6 11.9 bitcast_dynamic-update-slice_fusion
  449.5 4.9 fusion.53
  455.6 4.0 fusion.52
  461.5 3.5 pad_maximum_fusion.4
  465.0 5.0 all-to-all-start.4
  485.6 9.3 all-to-all-done.4
  497.8 4.1 copy.124
  502.0 3.9 reshape.510
  509.6 3.5 convolution_dynamic-update-slice_fusion.2
  518.7 16.5 %collective-permute-done = bf16[128,4608]{1,0:T(8,128)(2,1)S(1)} collective-permute-done((bf16[128,4608]{1,0:T(8,128)(2,1)S(1)}, bf16[128,4608]{1,0:T(8,128)(2,1)S(1)}, u32[]{:S(2)}, u32[]{:S(2)}) %collective-permute-start) | collective-permute-done | bytes 1179680 | tf_op jit(solution)/shard_map/ppermute | solution.py:18
  537.9 26.5 %collective-permute-done.1 = bf16[128,4608]{1,0:T(8,128)(2,1)S(1)} collective-permute-done((bf16[128,4608]{1,0:T(8,128)(2,1)S(1)}, bf16[128,4608]{1,0:T(8,128)(2,1)S(1)}, u32[]{:S(2)}, u32[]{:S(2)}) %collective-permute-start.1) | collective-permute-done | bytes 1179680 | tf_op jit(solution)/shard_map/ppermute | solution.py:18
  567.0 26.2 %collective-permute-done.2 = bf16[128,4608]{1,0:T(8,128)(2,1)} collective-permute-done((bf16[128,4608]{1,0:T(8,128)(2,1)S(1)}, bf16[128,4608]{1,0:T(8,128)(2,1)}, u32[]{:S(2)}, u32[]{:S(2)}) %collective-permute-start.2) | collective-permute-done | bytes 1179680 | tf_op jit(solution)/shard_map/ppermute | solution.py:18
  596.1 25.9 %collective-permute-done.3 = bf16[128,4608]{1,0:T(8,128)(2,1)} collective-permute-done((bf16[128,4608]{1,0:T(8,128)(2,1)}, bf16[128,4608]{1,0:T(8,128)(2,1)}, u32[]{:S(2)}, u32[]{:S(2)}) %collective-permute-start.3) | collective-permute-done | bytes 1179680 | tf_op jit(solution)/shard_map/ppermute | solution.py:18
  643.7 489.3 %reduce-scatter.2.cloned.1.call-done = f32[32,16896]{1,0:T(8,128)} async-done(((f32[1024,16896]{1,0:T(8,128)}), f32[32,16896]{1,0:T(8,128)}) %reduce-scatter.2.cloned.1.call-update) | async-done | bytes 2162704 | tf_op jit(solution)/shard_map/reduce_scatter | solution.py:80
  1144.0 10.4 add_convert_fusion
  1159.4 44.0 %all-reduce.2 = (f32[1024]{0:T(1024)}, f32[1024]{0:T(1024)}, f32[64]{0:T(128)}, f32[64]{0:T(128)}) all-reduce(f32[1024]{0:T(1024)S(1)} %get-tuple-element.81, f32[1024]{0:T(1024)S(1)} %get-tuple-element.79, f32[64]{0:T(128)S(1)} %get-tuple-element.77, f32[64]{0:T(128)S(1)} %get-tuple-element.83), channel_id=1, replica_groups=mesh['dp'=8,'seq'=4] {'dp','seq'}, use_global_device_ids=true, to_apply=%region_16.17 | all-reduce | flops 2176 | bytes 17408 | tf_op jit(solution)/shard_map/psum | solution.py:347
  1206.6 14.4 %all_gather.43 = bf16[128,1024]{1,0:T(8,128)(2,1)S(1)} all-gather(bf16[32,1024]{1,0:T(8,128)(2,1)S(1)} %slice-done), channel_id=1, replica_groups=mesh['dp'=8,'seq'=4] {'seq'}, dimensions={0}, use_global_device_ids=true | all-gather | bytes 327680 | tf_op jit(solution)/shard_map/all_gather | solution.py:340
  1221.8 14.7 %all_gather.42 = bf16[128,2048]{1,0:T(8,128)(2,1)S(1)} all-gather(bf16[32,2048]{1,0:T(8,128)(2,1)S(1)} %slice-done.1), channel_id=1, replica_groups=mesh['dp'=8,'seq'=4] {'seq'}, dimensions={0}, use_global_device_ids=true | all-gather | bytes 655360 | tf_op jit(solution)/shard_map/all_gather | solution.py:343
  1238.3 5.2 fusion.85
  (273 shorter events, 153.2 us)
Async XLA Ops:
  7.2 28.9 %all-gather.11.cloned.1.call-start = ((), (), s32[]{:S(2)}) async-start(), calls=%async_computation.8 | async-start | bytes 1179648 | tf_op jit(solution)/shard_map/all_gather | solution.py:127
  7.9 53.6 %all-gather.9.cloned.1.call-start = ((), (), s32[]{:S(2)}) async-start(), calls=%async_computation.7 | async-start | bytes 1179648 | tf_op jit(solution)/shard_map/all_gather | solution.py:126
  8.7 82.7 %all-gather.13.cloned.1.call-start = ((), (), s32[]{:S(2)}) async-start(), calls=%async_computation.9 | async-start | bytes 2359296 | tf_op jit(solution)/shard_map/all_gather | solution.py:125
  9.4 206.0 %all-gather.15.cloned.1.call-start = ((), (), s32[]{:S(2)}) async-start(), calls=%async_computation.10 | async-start | bytes 2359296 | tf_op jit(solution)/shard_map/all_gather | solution.py:128
  10.0 210.4 %all-gather.19.cloned.1.call-start = ((), (), s32[]{:S(2)}) async-start(), calls=%async_computation.12 | async-start | bytes 10616832 | tf_op jit(solution)/shard_map/all_gather | solution.py:207
  10.6 231.7 %all-gather.17.cloned.1.call-start = ((), (), s32[]{:S(2)}) async-start(), calls=%async_computation.11 | async-start | bytes 10616832 | tf_op jit(solution)/shard_map/all_gather | solution.py:206
  11.2 291.8 %all-gather.21.cloned.1.call-start = ((), (), s32[]{:S(2)}) async-start(), calls=%async_computation.13 | async-start | bytes 10616832 | tf_op jit(solution)/shard_map/all_gather | solution.py:218
  13.3 82.1 %copy-start.21 = (bf16[2,256,1024]{2,1,0:T(8,128)(2,1)}, bf16[2,256,1024]{2,1,0:T(8,128)(2,1)S(1)}, u32[]{:S(2)}) copy-start(bf16[2,256,1024]{2,1,0:T(8,128)(2,1)S(1)} %fusion.34) | copy-start | bytes 3145732
  13.9 86.1 %copy-start.37 = (f32[512,32]{0,1:T(8,128)}, f32[512,32]{0,1:T(8,128)S(1)}, u32[]{:S(2)}) copy-start(f32[512,32]{0,1:T(8,128)S(1)} %get-tuple-element.111) | copy-start | bytes 196612
  13.9 86.1 %copy-start.39 = (f32[512,32]{0,1:T(8,128)}, f32[512,32]{0,1:T(8,128)S(1)}, u32[]{:S(2)}) copy-start(f32[512,32]{0,1:T(8,128)S(1)} %get-tuple-element.112) | copy-start | bytes 196612
  38.9 25.9 %copy-start.61 = (f32[64]{0:T(128)S(1)}, f32[64]{0:T(128)}, u32[]{:S(2)}) copy-start(f32[64]{0:T(128)} %param.39) | copy-start | bytes 772
  68.0 33.6 %all-to-all-start = ((bf16[2,256,4,256]{3,1,0,2:T(8,128)(2,1)}), bf16[2,256,4,256]{3,1,0,2:T(8,128)(2,1)S(1)}, u32[]{:S(2)}, u32[]{:S(2)}) async-start(bf16[2,256,4,256]{3,1,0,2:T(8,128)(2,1)} %pad_maximum_fusion.1), calls=%async_computation | async-start | bytes 2097152 | tf_op jit(solution)/shard_map/all_to_all | solution.py:154
  101.6 31.0 %all-to-all-start.1 = ((bf16[2,256,4,256]{1,0,3,2:T(2,128)(2,1)}), bf16[2,256,4,256]{1,0,3,2:T(2,128)(2,1)S(1)}, u32[]{:S(2)}, u32[]{:S(2)}) async-start(bf16[2,256,4,256]{1,0,3,2:T(2,128)(2,1)} %convert_element_type.176), calls=%async_computation.1 | async-start | bytes 2097152 | tf_op jit(solution)/shard_map/all_to_all | solution.py:153
  134.1 9.8 copy-start.24
  151.6 10.6 copy-start.50
  162.2 9.8 copy-start.36
  174.4 39.8 %all-to-all-start.2 = ((bf16[2,1024,1,256]{3,0,2,1:T(2,128)(2,1)}), bf16[2,1024,1,256]{3,0,2,1:T(2,128)(2,1)S(1)}, u32[]{:S(2)}, u32[]{:S(2)}) async-start(bf16[2,1024,1,256]{3,0,2,1:T(2,128)(2,1)} %pad_maximum_fusion.3), calls=%async_computation.2 | async-start | bytes 2097152 | tf_op jit(solution)/shard_map/all_to_all | solution.py:200
  319.8 10.8 copy-start.19
  319.8 10.8 copy-start.9
  347.6 31.2 %all-to-all-start.3 = ((bf16[2,256,4,256]{1,3,0,2:T(8,128)(2,1)}), bf16[2,256,4,256]{1,3,0,2:T(8,128)(2,1)}, u32[]{:S(2)}, u32[]{:S(2)}) async-start(bf16[2,256,4,256]{1,3,0,2:T(8,128)(2,1)} %copy.117), calls=%async_computation.3 | async-start | bytes 2097152 | tf_op jit(solution)/shard_map/all_to_all | solution.py:230
  383.7 12.8 %copy-start.28 = (bf16[2,1024,2,2,64]{1,4,3,2,0:T(8,128)(2,1)}, bf16[2,1024,2,2,64]{1,4,3,2,0:T(8,128)(2,1)S(1)}, u32[]{:S(2)}) copy-start(bf16[2,1024,2,2,64]{1,4,3,2,0:T(8,128)(2,1)S(1)} %reshape.504) | copy-start | bytes 3145732
  405.4 13.2 %copy-start.25 = (bf16[2,1024,2,2,64]{1,4,3,2,0:T(8,128)(2,1)S(1)}, bf16[2,1024,2,2,64]{1,4,3,2,0:T(8,128)(2,1)}, u32[]{:S(2)}) copy-start(bf16[2,1024,2,2,64]{1,4,3,2,0:T(8,128)(2,1)} %copy-done.24) | copy-start | bytes 3145732
  433.4 31.7 %all-to-all-start.5 = ((bf16[2,1024,1,256]{3,0,2,1:T(2,128)(2,1)}), bf16[2,1024,1,256]{3,0,2,1:T(2,128)(2,1)}, u32[]{:S(2)}, u32[]{:S(2)}) async-start(bf16[2,1024,1,256]{3,0,2,1:T(2,128)(2,1)} %pad_maximum_fusion.5), calls=%async_computation.5 | async-start | bytes 2097152 | tf_op jit(solution)/shard_map/all_to_all | solution.py:280
  437.6 11.9 copy-start.30
  455.6 14.7 %copy-start.27 = (bf16[64,8,4,256]{3,1,2,0:T(8,128)(2,1)S(1)}, bf16[64,8,4,256]{3,1,2,0:T(8,128)(2,1)}, u32[]{:S(2)}) copy-start(bf16[64,8,4,256]{3,1,2,0:T(8,128)(2,1)} %copy-done.26) | copy-start | bytes 3145732
  465.0 29.9 %all-to-all-start.4 = ((bf16[2,1024,1,256]{3,0,2,1:T(2,128)(2,1)}), bf16[2,1024,1,256]{3,0,2,1:T(2,128)(2,1)}, u32[]{:S(2)}, u32[]{:S(2)}) async-start(bf16[2,1024,1,256]{3,0,2,1:T(2,128)(2,1)} %pad_maximum_fusion.4), calls=%async_computation.4 | async-start | bytes 2097152 | tf_op jit(solution)/shard_map/all_to_all | solution.py:279
  470.1 662.9 %reduce-scatter.2.cloned.1.call-start = ((), (), s32[]{:S(2)}) async-start(), calls=%async_computation.14 | async-start | bytes 71368704 | tf_op jit(solution)/shard_map/reduce_scatter | solution.py:80
  473.7 9.1 copy-start.38
  473.7 9.1 copy-start.40
  475.1 9.0 copy-start.6
  475.1 9.0 copy-start.53
  517.4 720.8 %all-gather.23.cloned.1.call-start = ((), (), s32[]{:S(2)}) async-start(), calls=%async_computation.15 | async-start | bytes 4423680 | tf_op jit(solution)/shard_map/all_gather | solution.py:337
  518.7 16.5 %collective-permute-start = (bf16[128,4608]{1,0:T(8,128)(2,1)S(1)}, bf16[128,4608]{1,0:T(8,128)(2,1)S(1)}, u32[]{:S(2)}, u32[]{:S(2)}) collective-permute-start(bf16[128,4608]{1,0:T(8,128)(2,1)S(1)} %copy-done.4), channel_id=1, source_target_pairs={{0,4},{4,8},{8,12},{12,16},{16,20},{20,24},{24,28},{28,0},{1,5},{5... | collective-permute-start | bytes 3538952 | tf_op jit(solution)/shard_map/ppermute | solution.py:18
  535.2 29.1 %copy-start.13 = (bf16[128,4608]{1,0:T(8,128)(2,1)}, bf16[128,4608]{1,0:T(8,128)(2,1)S(1)}, u32[]{:S(2)}) copy-start(bf16[128,4608]{1,0:T(8,128)(2,1)S(1)} %collective-permute-done) | copy-start | bytes 3538948
  535.2 29.1 %collective-permute-start.1 = (bf16[128,4608]{1,0:T(8,128)(2,1)S(1)}, bf16[128,4608]{1,0:T(8,128)(2,1)S(1)}, u32[]{:S(2)}, u32[]{:S(2)}) collective-permute-start(bf16[128,4608]{1,0:T(8,128)(2,1)S(1)} %collective-permute-done), channel_id=1, source_target_pairs={{0,4},{4,8},{8,12},{12,16},{16,20},{20,24},{24,28},{28,0},{1,5},{5... | collective-permute-start | bytes 3538952 | tf_op jit(solution)/shard_map/ppermute | solution.py:18
  535.2 29.1 %collective-permute-start.4 = (bf16[128,4608]{1,0:T(8,128)(2,1)S(1)}, bf16[128,4608]{1,0:T(8,128)(2,1)}, u32[]{:S(2)}, u32[]{:S(2)}) collective-permute-start(bf16[128,4608]{1,0:T(8,128)(2,1)S(1)} %copy-done.4), channel_id=1, source_target_pairs={{0,28},{4,0},{8,4},{12,8},{16,12},{20,16},{24,20},{28,24},{1,29},{... | collective-permute-start | bytes 3538952 | tf_op jit(solution)/shard_map/ppermute | solution.py:20
  564.3 28.8 %collective-permute-start.2 = (bf16[128,4608]{1,0:T(8,128)(2,1)S(1)}, bf16[128,4608]{1,0:T(8,128)(2,1)}, u32[]{:S(2)}, u32[]{:S(2)}) collective-permute-start(bf16[128,4608]{1,0:T(8,128)(2,1)S(1)} %collective-permute-done.1), channel_id=1, source_target_pairs={{0,4},{4,8},{8,12},{12,16},{16,20},{20,24},{24,28},{28,0},{1,5},{5... | collective-permute-start | bytes 3538952 | tf_op jit(solution)/shard_map/ppermute | solution.py:18
  564.4 28.8 %collective-permute-start.5 = (bf16[128,4608]{1,0:T(8,128)(2,1)}, bf16[128,4608]{1,0:T(8,128)(2,1)}, u32[]{:S(2)}, u32[]{:S(2)}) collective-permute-start(bf16[128,4608]{1,0:T(8,128)(2,1)} %collective-permute-done.4), channel_id=1, source_target_pairs={{0,28},{4,0},{8,4},{12,8},{16,12},{20,16},{24,20},{28,24},{1,29},{... | collective-permute-start | bytes 3538952 | tf_op jit(solution)/shard_map/ppermute | solution.py:20
  593.2 28.8 %collective-permute-start.3 = (bf16[128,4608]{1,0:T(8,128)(2,1)}, bf16[128,4608]{1,0:T(8,128)(2,1)}, u32[]{:S(2)}, u32[]{:S(2)}) collective-permute-start(bf16[128,4608]{1,0:T(8,128)(2,1)} %collective-permute-done.2), channel_id=1, source_target_pairs={{0,4},{4,8},{8,12},{12,16},{16,20},{20,24},{24,28},{28,0},{1,5},{5... | collective-permute-start | bytes 3538952 | tf_op jit(solution)/shard_map/ppermute | solution.py:18
  593.2 33.8 %copy-start.16 = (bf16[128,4608]{1,0:T(8,128)(2,1)S(1)}, bf16[128,4608]{1,0:T(8,128)(2,1)}, u32[]{:S(2)}) copy-start(bf16[128,4608]{1,0:T(8,128)(2,1)} %copy-done.15) | copy-start | bytes 3538948
  593.2 34.9 %copy-start.14 = (bf16[128,4608]{1,0:T(8,128)(2,1)S(1)}, bf16[128,4608]{1,0:T(8,128)(2,1)}, u32[]{:S(2)}) copy-start(bf16[128,4608]{1,0:T(8,128)(2,1)} %copy-done.13) | copy-start | bytes 3538948
  593.2 41.9 %collective-permute-start.6 = (bf16[128,4608]{1,0:T(8,128)(2,1)}, bf16[128,4608]{1,0:T(8,128)(2,1)S(1)}, u32[]{:S(2)}, u32[]{:S(2)}) collective-permute-start(bf16[128,4608]{1,0:T(8,128)(2,1)} %collective-permute-done.5), channel_id=1, source_target_pairs={{0,28},{4,0},{8,4},{12,8},{16,12},{20,16},{24,20},{28,24},{1,29},{... | collective-permute-start | bytes 3538952 | tf_op jit(solution)/shard_map/ppermute | solution.py:20
  1144.0 10.4 copy-start.12
  1144.0 10.4 copy-start.23
  1144.0 11.2 copy-start.35
  1144.0 11.2 copy-start.46
  1159.4 47.2 %slice-start = ((bf16[32,16896]{1,0:T(8,128)(2,1)}), bf16[32,1024]{1,0:T(8,128)(2,1)S(1)}, s32[]{:S(2)}) async-start(bf16[32,16896]{1,0:T(8,128)(2,1)} %copy-done.20), calls=%async_computation.16 | async-start | bytes 131072 | tf_op jit(solution)/shard_map/slice | solution.py:334
  1159.4 62.5 %slice-start.1 = ((bf16[32,16896]{1,0:T(8,128)(2,1)}), bf16[32,2048]{1,0:T(8,128)(2,1)S(1)}, s32[]{:S(2)}) async-start(bf16[32,16896]{1,0:T(8,128)(2,1)} %copy-done.20), calls=%async_computation.17 | async-start | bytes 262144 | tf_op jit(solution)/shard_map/slice | solution.py:335
  (40 other events, 160.2 us)
Sparse Core Ops, SparseCore 0:
  9.9 26.1 all-gather.10
  38.0 23.4 all-gather.8
  63.5 27.8 all-gather.12
  93.1 27.8 all-gather.14
  122.8 58.8 all-gather.18
  183.4 58.8 all-gather.16
  244.1 58.8 all-gather.20
  517.6 615.3 reduce-scatter.1
  1136.9 70.6 all-gather.22
